TPU v7x, 32 devices: a whole 2x2x4 slice. The times are simulated.
32 devices in a mesh: groups: 2 (over y), seq: 8 (over z, x), head: 1, sub: 2 (over core).
Axes of the slice: x: 2, y: 2, z: 4, core: 2. Of those that a mesh axis runs over, the one named last changes fastest.
Arguments:
- queries: bfloat16 [8, 32768, 512], P('head', ('groups', 'seq', 'sub')), parts along dimension 1, may hold values from -6 to 6
- keys: bfloat16 [8, 32768, 512], P('head', ('groups', 'seq', 'sub')), parts along dimension 1, may hold values from -6 to 6
- values: bfloat16 [8, 32768, 512], P('head', ('groups', 'seq', 'sub')), parts along dimension 1, may hold values from -6 to 6
- lr_codes: int32 [8, 32768], P('head', ('groups', 'seq', 'sub')), parts along dimension 1, may hold values from 0 to 15
- fast_gate: float32 [8, 512, 512], P('head', ('seq', 'sub')), may hold values from -0.25 to 0.25
- fast_up: float32 [8, 512, 512], P('head', ('seq', 'sub')), may hold values from -0.25 to 0.25
- fast_down: float32 [8, 512, 512], P('head', ('seq', 'sub')), may hold values from -0.25 to 0.25
Outputs:
- fast_out: bfloat16 [8, 32768, 512], P('head', ('groups', 'seq', 'sub')), parts along dimension 1
There are 2 independent parts, one for each index of `groups`. A program takes and returns all parts, laid end to end along the dimension named above; an argument that names none is the same for every part. Nothing has to cross between parts.
All inputs are finite; a program needn't handle non-finite values.
Results may differ from a plain program's by a relative error of at most 0.0085.
Values may be sent and summed in bfloat16 or wider, within the bound.
A program may use at most 192 MiB of HBM per device.

v0:
```python
import jax
import jax.numpy as jnp
from jax import lax
from jax.sharding import PartitionSpec as P

EPSILON = 1e-06
STEP_SIZE = 0.5


def column_squares(matrix):
    return jnp.sum(matrix * matrix, axis=1)


def rescale(moved, col_weight, col_moved):
    return moved * jnp.sqrt((col_weight + EPSILON) / (col_moved + EPSILON))[:, None, :]


def step_scale(col_weight, grad_total):
    return (
        STEP_SIZE * jnp.sqrt(jnp.sum(col_weight, axis=1) + EPSILON) / jnp.sqrt(grad_total + EPSILON)
    )


def apply_fast(queries, gate_b, up_b, down_b):
    query_gate = jnp.einsum("htd,hdf->htf", queries, gate_b, preferred_element_type=jnp.float32)
    query_up = jnp.einsum("htd,hdf->htf", queries, up_b, preferred_element_type=jnp.float32)
    query_hidden = (jax.nn.silu(query_gate) * query_up).astype(jnp.bfloat16)
    return jnp.einsum(
        "htf,hfd->htd", query_hidden, down_b, preferred_element_type=jnp.float32
    ).astype(jnp.bfloat16)


def local_grads(keys, target, gate_b, up_b, down_b):
    gate_pre = jnp.einsum("htd,hdf->htf", keys, gate_b, preferred_element_type=jnp.float32)
    up_pre = jnp.einsum("htd,hdf->htf", keys, up_b, preferred_element_type=jnp.float32)
    sigmoid_gate = jax.nn.sigmoid(gate_pre)
    hidden = (gate_pre * sigmoid_gate * up_pre).astype(jnp.bfloat16)
    back = jnp.einsum("htd,hfd->htf", target, down_b, preferred_element_type=jnp.float32)
    grad_gate_pre = (back * up_pre * sigmoid_gate * (1.0 + gate_pre * (1.0 - sigmoid_gate))).astype(
        jnp.bfloat16
    )
    grad_up_pre = (back * gate_pre * sigmoid_gate).astype(jnp.bfloat16)
    grad_gate = jnp.einsum("htd,htf->hdf", keys, grad_gate_pre, preferred_element_type=jnp.float32)
    grad_up = jnp.einsum("htd,htf->hdf", keys, grad_up_pre, preferred_element_type=jnp.float32)
    grad_down = jnp.einsum("htf,htd->hfd", hidden, target, preferred_element_type=jnp.float32)
    return (grad_gate, grad_up, grad_down)


def on_device(queries, keys, values, lr_codes, fast_gate, fast_up, fast_down):
    token_rates = (lr_codes.astype(jnp.float32) + 1.0) / 16.0
    target = (-token_rates[:, :, None] * values.astype(jnp.float32)).astype(jnp.bfloat16)
    gate_b, up_b, down_b = (
        lax.all_gather(fast_gate.astype(jnp.bfloat16), ("seq", "sub"), axis=1, tiled=True),
        lax.all_gather(fast_up.astype(jnp.bfloat16), ("seq", "sub"), axis=1, tiled=True),
        lax.all_gather(fast_down.astype(jnp.bfloat16), ("seq", "sub"), axis=1, tiled=True),
    )
    grad_gate, grad_up, grad_down = local_grads(keys, target, gate_b, up_b, down_b)
    owned = (
        lax.psum_scatter(grad_gate, ("seq", "sub"), scatter_dimension=1, tiled=True),
        lax.psum_scatter(grad_up, ("seq", "sub"), scatter_dimension=1, tiled=True),
        lax.psum_scatter(grad_down, ("seq", "sub"), scatter_dimension=1, tiled=True),
    )
    weights = (fast_gate, fast_up, fast_down)
    grad_local = jnp.stack(
        [
            jnp.sum(owned[0] * owned[0], axis=(1, 2)),
            jnp.sum(owned[1] * owned[1], axis=(1, 2)),
            jnp.sum(owned[2] * owned[2], axis=(1, 2)),
        ],
        axis=1,
    )
    col_gate, col_up, col_down, grad_totals = lax.psum(
        (column_squares(fast_gate), column_squares(fast_up), column_squares(fast_down), grad_local),
        ("seq", "sub"),
    )
    col_weights = (col_gate, col_up, col_down)
    moved_all = []
    for index in range(3):
        scale = step_scale(col_weights[index], grad_totals[:, index])
        moved_all.append(weights[index] - scale[:, None, None] * owned[index])
    moved_cols = lax.psum(
        (column_squares(moved_all[0]), column_squares(moved_all[1]), column_squares(moved_all[2])),
        ("seq", "sub"),
    )
    renewed = [
        rescale(moved_all[index], col_weights[index], moved_cols[index]).astype(jnp.bfloat16)
        for index in range(3)
    ]
    new_gate, new_up, new_down = (
        lax.all_gather(renewed[0], ("seq", "sub"), axis=1, tiled=True),
        lax.all_gather(renewed[1], ("seq", "sub"), axis=1, tiled=True),
        lax.all_gather(renewed[2], ("seq", "sub"), axis=1, tiled=True),
    )
    return apply_fast(queries, new_gate, new_up, new_down)


def solution(mesh):
    return jax.shard_map(
        on_device,
        mesh=mesh,
        in_specs=(
            P("head", ("groups", "seq", "sub"), None),
            P("head", ("groups", "seq", "sub"), None),
            P("head", ("groups", "seq", "sub"), None),
            P("head", ("groups", "seq", "sub")),
            P("head", ("seq", "sub"), None),
            P("head", ("seq", "sub"), None),
            P("head", ("seq", "sub"), None),
        ),
        out_specs=P("head", ("groups", "seq", "sub"), None),
        check_vma=False,
    )
```

profile of v0, /device:TPU:0, one launch (start us, length us, event | category | flops | bytes accessed | tf_op | source)
XLA Modules:
  0.0 794.0 jit_solution(1773407533182401554)
XLA Ops:
  6.5 2.6 multiply_reduce_fusion.8
  9.2 2.6 multiply_reduce_fusion.1
  11.8 2.6 multiply_reduce_fusion.3
  15.3 47.5 %all-gather.11.cloned.1.call-done = bf16[8,512,512]{2,1,0:T(8,128)(2,1)} async-done(((bf16[8,32,512]{2,1,0:T(8,128)(2,1)}), bf16[8,512,512]{2,1,0:T(8,128)(2,1)}) %all-gather.11.cloned.1.call-update) | async-done | bytes 4194320 | tf_op jit(solution)/shard_map/all_gather | solution.py:53
  62.9 14.8 %fusion.19 = f32[8,1024,512]{2,1,0:T(8,128)} fusion(bf16[8,1024,512]{2,1,0:T(8,128)(2,1)} %param.8, bf16[8,512,512]{2,1,0:T(8,128)(2,1)} %all-gather.11.cloned.1.call-done), kind=kOutput, calls=%fused_computation.50 | convolution fusion | flops 4294967296 | bytes 29360128 | tf_op jit(solution)/shard_map/htd,hdf->htf/dot_general | solution.py:34
  77.7 36.5 %all-gather.7.cloned.1.call-done = bf16[8,512,512]{2,1,0:T(8,128)(2,1)} async-done(((bf16[8,32,512]{2,1,0:T(8,128)(2,1)}), bf16[8,512,512]{2,1,0:T(8,128)(2,1)}) %all-gather.7.cloned.1.call-update) | async-done | bytes 4194320 | tf_op jit(solution)/shard_map/all_gather | solution.py:55
  114.1 11.7 %fusion.7 = f32[8,1024,512]{2,1,0:T(8,128)} fusion(bf16[8,512,512]{2,1,0:T(8,128)(2,1)} %all-gather.7.cloned.1.call-done, bf16[8,1024,512]{2,1,0:T(8,128)(2,1)} %param.9, f32[8,1024]{1,0:T(8,128)S(1)} %multiply_negate_fusion), kind=kOutput, calls=%fused_computation.15 | convolution fusion | flops 4307550208 | bytes 29392896 | tf_op jit(solution)/shard_map/htd,hfd->htf/dot_general | solution.py:38
  125.8 19.5 %fusion.13 = f32[8,512,512]{1,2,0:T(8,128)} fusion(bf16[8,1024,512]{2,1,0:T(8,128)(2,1)} %param.8, f32[8,1024,512]{2,1,0:T(8,128)} %fusion.7, f32[8,1024,512]{2,1,0:T(8,128)} %fusion.19), kind=kOutput, calls=%fused_computation.21 | convolution fusion | flops 4320133120 | bytes 50331648 | tf_op jit(solution)/shard_map/htd,htf->hdf/dot_general | solution.py:44
  145.3 10.5 %copy.18 = f32[8,512,512]{2,0,1:T(8,128)} copy(f32[8,512,512]{1,2,0:T(8,128)} %fusion.13) | data formatting | bytes 16777216 | tf_op jit(solution)/shard_map/htd,htf->hdf/dot_general | solution.py:44
  156.0 9.4 %all-gather.9.cloned.1.call-done = bf16[8,512,512]{2,1,0:T(8,128)(2,1)} async-done(((bf16[8,32,512]{2,1,0:T(8,128)(2,1)}), bf16[8,512,512]{2,1,0:T(8,128)(2,1)}) %all-gather.9.cloned.1.call-update) | async-done | bytes 4194320 | tf_op jit(solution)/shard_map/all_gather | solution.py:54
  165.4 16.6 %fusion.18 = f32[8,1024,512]{2,1,0:T(8,128)} fusion(bf16[8,1024,512]{2,1,0:T(8,128)(2,1)} %param.8, bf16[8,512,512]{2,1,0:T(8,128)(2,1)} %all-gather.9.cloned.1.call-done), kind=kOutput, calls=%fused_computation.49 | convolution fusion | flops 4294967296 | bytes 29360128 | tf_op jit(solution)/shard_map/htd,hdf->htf/dot_general | solution.py:35
  182.0 21.8 %fusion.5 = f32[8,512,512]{2,1,0:T(8,128)} fusion(f32[8,1024,512]{2,1,0:T(8,128)} %fusion.18, f32[8,1024,512]{2,1,0:T(8,128)} %fusion.19, bf16[8,1024,512]{2,1,0:T(8,128)(2,1)} %param.9, f32[8,1024]{1,0:T(8,128)S(1)} %multiply_negate_fusion), kind=kOutput, calls=%fused_computation.13 | convolution fusion | flops 4332716032 | bytes 50364416 | tf_op jit(solution)/shard_map/htf,htd->hfd/dot_general | solution.py:45
  203.9 25.5 %fusion.12 = f32[8,512,512]{1,2,0:T(8,128)} fusion(bf16[8,1024,512]{2,1,0:T(8,128)(2,1)} %param.8, f32[8,1024,512]{2,1,0:T(8,128)} %fusion.19, f32[8,1024,512]{2,1,0:T(8,128)} %fusion.7, f32[8,1024,512]{2,1,0:T(8,128)} %fusion.18), kind=kOutput, calls=%fused_computation.20 | convolution fusion | flops 4336910336 | bytes 67108864 | tf_op jit(solution)/shard_map/htd,htf->hdf/dot_general | solution.py:43
  229.4 10.6 %copy.16 = f32[8,512,512]{2,0,1:T(8,128)} copy(f32[8,512,512]{1,2,0:T(8,128)} %fusion.12) | data formatting | bytes 16777216 | tf_op jit(solution)/shard_map/htd,htf->hdf/dot_general | solution.py:43
  240.1 32.5 %reduce-scatter.6.cloned.1.call-done = f32[8,32,512]{2,0,1:T(8,128)} async-done(((f32[8,512,512]{2,0,1:T(8,128)}), f32[8,32,512]{2,0,1:T(8,128)}) %reduce-scatter.6.cloned.1.call-update) | async-done | bytes 524304 | tf_op jit(solution)/shard_map/reduce_scatter | solution.py:60
  272.6 1.4 multiply_reduce_fusion.6
  273.9 107.0 %reduce-scatter.8.cloned.1.call-done = f32[8,32,512]{2,1,0:T(8,128)} async-done(((f32[8,512,512]{2,1,0:T(8,128)}), f32[8,32,512]{2,1,0:T(8,128)}) %reduce-scatter.8.cloned.1.call-update) | async-done | bytes 524304 | tf_op jit(solution)/shard_map/reduce_scatter | solution.py:61
  381.0 1.2 multiply_reduce_fusion.5
  382.2 107.2 %reduce-scatter.4.cloned.1.call-done = f32[8,32,512]{2,0,1:T(8,128)} async-done(((f32[8,512,512]{2,0,1:T(8,128)}), f32[8,32,512]{2,0,1:T(8,128)}) %reduce-scatter.4.cloned.1.call-update) | async-done | bytes 524304 | tf_op jit(solution)/shard_map/reduce_scatter | solution.py:59
  489.3 1.3 multiply_reduce_fusion.7
  490.7 60.4 %all-reduce.1 = (f32[8,3]{0,1:T(4,128)S(1)}, f32[8,512]{1,0:T(8,128)S(1)}, f32[8,512]{1,0:T(8,128)S(1)}, f32[8,512]{1,0:T(8,128)S(1)}) all-reduce(f32[8,3]{0,1:T(4,128)S(1)} %pad_maximum_fusion, f32[8,512]{1,0:T(8,128)S(1)} %copy-done.5, ...), channel_id=1, replica_groups=mesh['groups'=2,'seq'=8,'head'=1,'sub'=2] {'seq','sub'}, use_global_device_ids=true, to_apply=%region_9.0 | all-reduce | flops 12312 | bytes 98496 | tf_op jit(solution)/shard_map/psum | solution.py:72
  551.4 1.2 multiply_reduce_fusion
  552.7 1.9 multiply_reduce_fusion.2
  554.6 57.7 %all-reduce = (f32[8,512]{1,0:T(8,128)S(1)}, f32[8,512]{1,0:T(8,128)S(1)}, f32[8,512]{1,0:T(8,128)S(1)}) all-reduce(f32[8,512]{1,0:T(8,128)S(1)} %multiply_reduce_fusion, f32[8,512]{1,0:T(8,128)S(1)} %get-tuple-element.22, f32[8,512]{1,0:T(8,128)S(1)} %get-tuple-element.21), channel_id=1, replica_groups=mesh['groups'=2,'seq'=8,'head'=1,'sub'=2] {'seq','sub'}, use_global_device_ids=true, to_apply=%region_21.0 | all-reduce | flops 12288 | bytes 98304 | tf_op jit(solution)/shard_map/psum | solution.py:81
  612.3 2.1 multiply_convert_fusion.15
  614.5 1.9 multiply_convert_fusion.13
  616.7 1.0 multiply_convert_fusion.14
  617.7 44.6 %all-gather.13.cloned.1.call-done = bf16[8,512,512]{2,0,1:T(8,128)(2,1)} async-done(((bf16[8,32,512]{2,0,1:T(8,128)(2,1)}), bf16[8,512,512]{2,0,1:T(8,128)(2,1)}) %all-gather.13.cloned.1.call-update) | async-done | bytes 4194320 | tf_op jit(solution)/shard_map/all_gather | solution.py:90
  662.3 14.9 %fusion.10 = f32[8,512,1024]{1,2,0:T(8,128)} fusion(bf16[8,1024,512]{2,1,0:T(8,128)(2,1)} %param.7, bf16[8,512,512]{2,0,1:T(8,128)(2,1)} %all-gather.13.cloned.1.call-done), kind=kOutput, calls=%fused_computation.18 | convolution fusion | flops 4294967296 | bytes 29360128 | tf_op jit(solution)/shard_map/htd,hdf->htf/dot_general | solution.py:25
  677.3 36.4 %all-gather.17.cloned.1.call-done = bf16[8,512,512]{2,1,0:T(8,128)(2,1)} async-done(((bf16[8,32,512]{2,1,0:T(8,128)(2,1)}), bf16[8,512,512]{2,1,0:T(8,128)(2,1)}) %all-gather.17.cloned.1.call-update) | async-done | bytes 4194320 | tf_op jit(solution)/shard_map/all_gather | solution.py:92
  713.6 51.2 %all-gather.15.cloned.1.call-done = bf16[8,512,512]{2,0,1:T(8,128)(2,1)} async-done(((bf16[8,32,512]{2,0,1:T(8,128)(2,1)}), bf16[8,512,512]{2,0,1:T(8,128)(2,1)}) %all-gather.15.cloned.1.call-update) | async-done | bytes 4194320 | tf_op jit(solution)/shard_map/all_gather | solution.py:91
  764.9 22.5 %convolution_convert_fusion = bf16[8,1024,512]{2,1,0:T(8,128)(2,1)} fusion(bf16[8,512,512]{2,1,0:T(8,128)(2,1)} %all-gather.17.cloned.1.call-done, f32[8,512,1024]{1,2,0:T(8,128)} %fusion.10, bf16[8,1024,512]{2,1,0:T(8,128)(2,1)} %param.7, bf16[8,512,512]{2,0,1:T(8,128)(2,1)} %all-gather.15.cloned.1.call-done), kind=kOutput, calls=%fused_computation.16 | convolution fusion | flops 8619294720 | bytes 41943040 | tf_op jit(solution)/shard_map/htf,hfd->htd/dot_general | solution.py:28
  (41 shorter events, 2.1 us)
Async XLA Ops:
  6.5 56.3 %all-gather.11.cloned.1.call-start = ((), (), s32[]{:S(2)}) async-start(), calls=%async_computation.5 | async-start | bytes 4456448 | tf_op jit(solution)/shard_map/all_gather | solution.py:53
  9.1 105.0 %all-gather.7.cloned.1.call-start = ((), (), s32[]{:S(2)}) async-start(), calls=%async_computation.3 | async-start | bytes 4456448 | tf_op jit(solution)/shard_map/all_gather | solution.py:55
  11.8 153.7 %all-gather.9.cloned.1.call-start = ((), (), s32[]{:S(2)}) async-start(), calls=%async_computation.4 | async-start | bytes 4456448 | tf_op jit(solution)/shard_map/all_gather | solution.py:54
  14.5 258.1 %reduce-scatter.6.cloned.1.call-start = ((), (), s32[]{:S(2)}) async-start(), calls=%async_computation.7 | async-start | bytes 8912896 | tf_op jit(solution)/shard_map/reduce_scatter | solution.py:60
  155.8 225.2 %reduce-scatter.8.cloned.1.call-start = ((), (), s32[]{:S(2)}) async-start(), calls=%async_computation.8 | async-start | bytes 8912896 | tf_op jit(solution)/shard_map/reduce_scatter | solution.py:61
  203.8 285.5 %reduce-scatter.4.cloned.1.call-start = ((), (), s32[]{:S(2)}) async-start(), calls=%async_computation.6 | async-start | bytes 8912896 | tf_op jit(solution)/shard_map/reduce_scatter | solution.py:59
  240.0 250.7 %copy-start.4 = (f32[8,512]{1,0:T(8,128)S(1)}, f32[8,512]{1,0:T(8,128)}, u32[]{:S(2)}) copy-start(f32[8,512]{1,0:T(8,128)} %get-tuple-element.14) | copy-start | bytes 49156
  240.0 250.7 %copy-start.5 = (f32[8,512]{1,0:T(8,128)S(1)}, f32[8,512]{1,0:T(8,128)}, u32[]{:S(2)}) copy-start(f32[8,512]{1,0:T(8,128)} %get-tuple-element.16) | copy-start | bytes 49156
  240.0 250.7 %copy-start.6 = (f32[8,512]{1,0:T(8,128)S(1)}, f32[8,512]{1,0:T(8,128)}, u32[]{:S(2)}) copy-start(f32[8,512]{1,0:T(8,128)} %get-tuple-element.12) | copy-start | bytes 49156
  240.0 311.4 %copy-start = (f32[8,32,512]{2,1,0:T(8,128)S(1)}, f32[8,32,512]{2,1,0:T(8,128)}, u32[]{:S(2)}) copy-start(f32[8,32,512]{2,1,0:T(8,128)} %param.13) | copy-start | bytes 1572868
  240.0 312.7 %copy-start.1 = (f32[8,32,512]{2,1,0:T(8,128)S(1)}, f32[8,32,512]{2,1,0:T(8,128)}, u32[]{:S(2)}) copy-start(f32[8,32,512]{2,1,0:T(8,128)} %param.11) | copy-start | bytes 1572868
  240.0 312.7 %copy-start.2 = (f32[8,32,512]{2,1,0:T(8,128)S(1)}, f32[8,32,512]{2,1,0:T(8,128)}, u32[]{:S(2)}) copy-start(f32[8,32,512]{2,1,0:T(8,128)} %param.12) | copy-start | bytes 1572868
  240.0 422.3 %all-gather.13.cloned.1.call-start = ((), (), s32[]{:S(2)}) async-start(), calls=%async_computation.9 | async-start | bytes 4456448 | tf_op jit(solution)/shard_map/all_gather | solution.py:90
  272.6 344.1 %copy-start.3 = (f32[8,32,512]{2,0,1:T(8,128)S(1)}, f32[8,32,512]{2,0,1:T(8,128)}, u32[]{:S(2)}) copy-start(f32[8,32,512]{2,0,1:T(8,128)} %reduce-scatter.6.cloned.1.call-done) | copy-start | bytes 1572868
  614.4 99.2 %all-gather.17.cloned.1.call-start = ((), (), s32[]{:S(2)}) async-start(), calls=%async_computation.11 | async-start | bytes 4456448 | tf_op jit(solution)/shard_map/all_gather | solution.py:92
  616.4 148.5 %all-gather.15.cloned.1.call-start = ((), (), s32[]{:S(2)}) async-start(), calls=%async_computation.10 | async-start | bytes 4456448 | tf_op jit(solution)/shard_map/all_gather | solution.py:91
Sparse Core Ops, SparseCore 0:
  9.5 53.2 all-gather.10
  65.0 49.0 all-gather.6
  116.3 49.0 all-gather.8
  169.4 103.1 reduce-scatter.5
  276.5 104.4 reduce-scatter.7
  384.9 104.4 reduce-scatter.3
  614.5 47.7 all-gather.12
  664.5 49.0 all-gather.16
  715.8 49.0 all-gather.14
where the time goes:
time: 795 us; the launch traced here: 794 us
  waiting for transfers between devices  472 us (59%)
  matrix products  147 us (18%)
  blocking collectives  118 us (15%)
  local copies, waits for them, and re-layouts  21.1 us (3%)
  other arithmetic  20.9 us (3%)
  between operations  13.3 us (2%)
    reduce_scatter x1, waiting for transfers between devices, on_device(): lax.psum_scatter(grad_gate, ('seq', 'sub'), scatter_dimension=1, tiled=True)  107 us
    reduce_scatter x1, waiting for transfers between devices, on_device(): lax.psum_scatter(grad_down, ('seq', 'sub'), scatter_dimension=1, tiled=True)  107 us
    psum x1, blocking collectives, on_device(): lax.psum((column_squares(fast_gate), column_squares(fast_up), column_squa...  60.4 us
    psum x1, blocking collectives, on_device(): lax.psum((column_squares(moved_all[0]), column_squares(moved_all[1]), col...  57.7 us
    all_gather x1, waiting for transfers between devices, on_device(): lax.all_gather(renewed[1], ('seq', 'sub'), axis=1, tiled=True)  51.2 us
    all_gather x1, waiting for transfers between devices, on_device(): lax.all_gather(fast_gate.astype(jnp.bfloat16), ('seq', 'sub'), axis=1, ti...  47.5 us
    all_gather x1, waiting for transfers between devices, on_device(): lax.all_gather(renewed[0], ('seq', 'sub'), axis=1, tiled=True)  44.6 us
    all_gather x1, waiting for transfers between devices, on_device(): lax.all_gather(fast_down.astype(jnp.bfloat16), ('seq', 'sub'), axis=1, ti...  36.5 us
  transfers between devices with their start and end apart: 9, of which 9 were waited for; matrix products, arithmetic and copies ran while one was open for 20% of the time, Pallas kernels for 0%

commit v1 on v0

--- a/solution.py
+++ b/solution.py
@@ -5,6 +5,29 @@
 
 EPSILON = 1e-06
 STEP_SIZE = 0.5
+
+
+def _link_racks(a0):
+    r_now = lax.axis_size(("seq", "sub"))
+    u_next = lax.axis_index(("seq", "sub"))
+    z1, mixed_arr, far_arr = (r_now, u_next, a0.shape[1])
+    sheets = [(j0, (j0 + 1) % z1) for j0 in range(z1)]
+    latest = jnp.zeros((*a0.shape[:1], z1 * far_arr, *a0.shape[2:]), a0.dtype)
+    latest = lax.dynamic_update_slice_in_dim(latest, a0, mixed_arr * far_arr, axis=1)
+    pages = [(j0, (j0 - 1) % z1) for j0 in range(z1)]
+    z2 = heard = a0
+    answer = z1 // 2
+    for jj in range(1, answer + 1):
+        z2 = lax.ppermute(z2, ("seq", "sub"), perm=sheets)
+        latest = lax.dynamic_update_slice_in_dim(
+            latest, z2, (mixed_arr - jj) % z1 * far_arr, axis=1
+        )
+        if jj < z1 - answer:
+            heard = lax.ppermute(heard, axis_name=("seq", "sub"), perm=pages)
+            latest = lax.dynamic_update_slice_in_dim(
+                latest, heard, (mixed_arr + jj) % z1 * far_arr, axis=1
+            )
+    return latest
 
 
 def column_squares(matrix):
@@ -89,7 +112,7 @@
     new_gate, new_up, new_down = (
         lax.all_gather(renewed[0], ("seq", "sub"), axis=1, tiled=True),
         lax.all_gather(renewed[1], ("seq", "sub"), axis=1, tiled=True),
-        lax.all_gather(renewed[2], ("seq", "sub"), axis=1, tiled=True),
+        _link_racks(renewed[2]),
     )
     return apply_fast(queries, new_gate, new_up, new_down)
 

time: 795 us -> 760 us (0.956)
  waiting for transfers between devices: 472 us -> 392 us
  starting transfers between devices: 0.74 us -> 32.2 us
  local copies, waits for them, and re-layouts: 21.1 us -> 34.8 us
    all_gather x1, waiting for transfers between devices: 44.6 us -> 0.01 us  [on_device(): lax.all_gather(renewed[0], ('seq', 'sub'), axis=1, tiled=True)]
    ppermute x0 -> x15, waiting for transfers between devices: none -> 41.4 us  [the longest x8 30.8 us: _link_racks(): z2 = lax.ppermute(z2, ('seq', 'sub'), perm=sheets)]
    all_gather x1, waiting for transfers between devices: 51.2 us -> 10.8 us  [on_device(): lax.all_gather(renewed[1], ('seq', 'sub'), axis=1, tiled=True)]
    all_gather x1 -> x0, waiting for transfers between devices: 36.4 us -> none  [on_device(): lax.all_gather(renewed[2], ('seq', 'sub'), axis=1, tiled=True)]
    ppermute x0 -> x15, starting transfers between devices: none -> 31.7 us  [the longest x7 31.7 us: _link_racks(): heard = lax.ppermute(heard, axis_name=('seq', 'sub'), perm=pages)]
    dynamic_update_slice x0 -> x15, local copies, waits for them, and re-layouts: none -> 11.4 us  [the longest x8 6.01 us: _link_racks(): lax.dynamic_update_slice_in_dim(latest, z2, (mixed_arr - jj) % z1 * far_a...]
  transfers between devices with their start and end apart: 9 -> 23, of which waited for: 9 -> 19; matrix products, arithmetic and copies ran while one was open for 20% -> 22% of each run, Pallas kernels for 0% -> 0%
where the time goes in v1:
time: 760 us; the launch traced here: 759 us
  waiting for transfers between devices  392 us (52%)
  matrix products  148 us (19%)
  blocking collectives  118 us (16%)
  local copies, waits for them, and re-layouts  34.8 us (5%)
  starting transfers between devices  32.2 us (4%)
  other arithmetic  20.3 us (3%)
  between operations  13.7 us (2%)
    reduce_scatter x1, waiting for transfers between devices, on_device(): lax.psum_scatter(grad_down, ('seq', 'sub'), scatter_dimension=1, tiled=True)  107 us
    reduce_scatter x1, waiting for transfers between devices, on_device(): lax.psum_scatter(grad_gate, ('seq', 'sub'), scatter_dimension=1, tiled=True)  107 us
    psum x1, blocking collectives, on_device(): lax.psum((column_squares(fast_gate), column_squares(fast_up), column_squa...  60.4 us
    psum x1, blocking collectives, on_device(): lax.psum((column_squares(moved_all[0]), column_squares(moved_all[1]), col...  57.7 us
    all_gather x1, waiting for transfers between devices, on_device(): lax.all_gather(fast_gate.astype(jnp.bfloat16), ('seq', 'sub'), axis=1, ti...  47.5 us
    all_gather x1, waiting for transfers between devices, on_device(): lax.all_gather(fast_down.astype(jnp.bfloat16), ('seq', 'sub'), axis=1, ti...  36.5 us
    reduce_scatter x1, waiting for transfers between devices, on_device(): lax.psum_scatter(grad_up, ('seq', 'sub'), scatter_dimension=1, tiled=True)  32.6 us
    ppermute x7, starting transfers between devices, _link_racks(): heard = lax.ppermute(heard, axis_name=('seq', 'sub'), perm=pages)  31.7 us
  transfers between devices with their start and end apart: 23, of which 19 were waited for; matrix products, arithmetic and copies ran while one was open for 22% of the time, Pallas kernels for 0%

profile of v1, /device:TPU:0, one launch (start us, length us, event | category | flops | bytes accessed | tf_op | source)
XLA Modules:
  0.0 759.2 jit_solution(16999665065831587419)
XLA Ops:
  15.3 47.5 %all-gather.10.cloned.1.call-done = bf16[8,512,512]{2,1,0:T(8,128)(2,1)} async-done(((bf16[8,32,512]{2,1,0:T(8,128)(2,1)}), bf16[8,512,512]{2,1,0:T(8,128)(2,1)}) %all-gather.10.cloned.1.call-update) | async-done | bytes 4194320 | tf_op jit(solution)/shard_map/all_gather | solution.py:76
  62.9 14.8 %fusion.19 = f32[8,1024,512]{2,1,0:T(8,128)} fusion(bf16[8,1024,512]{2,1,0:T(8,128)(2,1)} %param.8, bf16[8,512,512]{2,1,0:T(8,128)(2,1)} %all-gather.10.cloned.1.call-done), kind=kOutput, calls=%fused_computation.66 | convolution fusion | flops 4294967296 | bytes 29360128 | tf_op jit(solution)/shard_map/htd,hdf->htf/dot_general | solution.py:57
  77.7 36.5 %all-gather.6.cloned.1.call-done = bf16[8,512,512]{2,1,0:T(8,128)(2,1)} async-done(((bf16[8,32,512]{2,1,0:T(8,128)(2,1)}), bf16[8,512,512]{2,1,0:T(8,128)(2,1)}) %all-gather.6.cloned.1.call-update) | async-done | bytes 4194320 | tf_op jit(solution)/shard_map/all_gather | solution.py:78
  114.1 11.7 %fusion.7 = f32[8,1024,512]{2,1,0:T(8,128)} fusion(bf16[8,512,512]{2,1,0:T(8,128)(2,1)} %all-gather.6.cloned.1.call-done, bf16[8,1024,512]{2,1,0:T(8,128)(2,1)} %param.9, f32[8,1024]{1,0:T(8,128)S(1)} %multiply_negate_fusion), kind=kOutput, calls=%fused_computation.15 | convolution fusion | flops 4307550208 | bytes 29392896 | tf_op jit(solution)/shard_map/htd,hfd->htf/dot_general | solution.py:61
  125.8 19.5 %fusion.13 = f32[8,512,512]{1,2,0:T(8,128)} fusion(bf16[8,1024,512]{2,1,0:T(8,128)(2,1)} %param.8, f32[8,1024,512]{2,1,0:T(8,128)} %fusion.7, f32[8,1024,512]{2,1,0:T(8,128)} %fusion.19), kind=kOutput, calls=%fused_computation.21 | convolution fusion | flops 4320133120 | bytes 50331648 | tf_op jit(solution)/shard_map/htd,htf->hdf/dot_general | solution.py:67
  145.3 10.5 %copy.18 = f32[8,512,512]{2,0,1:T(8,128)} copy(f32[8,512,512]{1,2,0:T(8,128)} %fusion.13) | data formatting | bytes 16777216 | tf_op jit(solution)/shard_map/htd,htf->hdf/dot_general | solution.py:67
  156.0 9.4 %all-gather.8.cloned.1.call-done = bf16[8,512,512]{2,1,0:T(8,128)(2,1)} async-done(((bf16[8,32,512]{2,1,0:T(8,128)(2,1)}), bf16[8,512,512]{2,1,0:T(8,128)(2,1)}) %all-gather.8.cloned.1.call-update) | async-done | bytes 4194320 | tf_op jit(solution)/shard_map/all_gather | solution.py:77
  165.4 16.6 %fusion.18 = f32[8,1024,512]{2,1,0:T(8,128)} fusion(bf16[8,1024,512]{2,1,0:T(8,128)(2,1)} %param.8, bf16[8,512,512]{2,1,0:T(8,128)(2,1)} %all-gather.8.cloned.1.call-done), kind=kOutput, calls=%fused_computation.65 | convolution fusion | flops 4294967296 | bytes 29360128 | tf_op jit(solution)/shard_map/htd,hdf->htf/dot_general | solution.py:58
  182.0 21.8 %fusion.5 = f32[8,512,512]{2,1,0:T(8,128)} fusion(f32[8,1024,512]{2,1,0:T(8,128)} %fusion.18, f32[8,1024,512]{2,1,0:T(8,128)} %fusion.19, bf16[8,1024,512]{2,1,0:T(8,128)(2,1)} %param.9, f32[8,1024]{1,0:T(8,128)S(1)} %multiply_negate_fusion), kind=kOutput, calls=%fused_computation.13 | convolution fusion | flops 4332716032 | bytes 50364416 | tf_op jit(solution)/shard_map/htf,htd->hfd/dot_general | solution.py:68
  203.9 25.5 %fusion.12 = f32[8,512,512]{1,2,0:T(8,128)} fusion(bf16[8,1024,512]{2,1,0:T(8,128)(2,1)} %param.8, f32[8,1024,512]{2,1,0:T(8,128)} %fusion.19, f32[8,1024,512]{2,1,0:T(8,128)} %fusion.7, f32[8,1024,512]{2,1,0:T(8,128)} %fusion.18), kind=kOutput, calls=%fused_computation.20 | convolution fusion | flops 4336910336 | bytes 67108864 | tf_op jit(solution)/shard_map/htd,htf->hdf/dot_general | solution.py:66
  229.4 10.6 %copy.16 = f32[8,512,512]{2,0,1:T(8,128)} copy(f32[8,512,512]{1,2,0:T(8,128)} %fusion.12) | data formatting | bytes 16777216 | tf_op jit(solution)/shard_map/htd,htf->hdf/dot_general | solution.py:66
  240.0 32.6 %reduce-scatter.6.cloned.1.call-done = f32[8,32,512]{2,0,1:T(8,128)} async-done(((f32[8,512,512]{2,0,1:T(8,128)}), f32[8,32,512]{2,0,1:T(8,128)}) %reduce-scatter.6.cloned.1.call-update) | async-done | bytes 524304 | tf_op jit(solution)/shard_map/reduce_scatter | solution.py:83
  273.9 107.1 %reduce-scatter.8.cloned.1.call-done = f32[8,32,512]{2,1,0:T(8,128)} async-done(((f32[8,512,512]{2,1,0:T(8,128)}), f32[8,32,512]{2,1,0:T(8,128)}) %reduce-scatter.8.cloned.1.call-update) | async-done | bytes 524304 | tf_op jit(solution)/shard_map/reduce_scatter | solution.py:84
  382.3 107.0 %reduce-scatter.4.cloned.1.call-done = f32[8,32,512]{2,0,1:T(8,128)} async-done(((f32[8,512,512]{2,0,1:T(8,128)}), f32[8,32,512]{2,0,1:T(8,128)}) %reduce-scatter.4.cloned.1.call-update) | async-done | bytes 524304 | tf_op jit(solution)/shard_map/reduce_scatter | solution.py:82
  490.6 60.4 %all-reduce.1 = (f32[8,3]{0,1:T(4,128)S(1)}, f32[8,512]{1,0:T(8,128)S(1)}, f32[8,512]{1,0:T(8,128)S(1)}, f32[8,512]{1,0:T(8,128)S(1)}) all-reduce(f32[8,3]{0,1:T(4,128)S(1)} %pad_maximum_fusion, f32[8,512]{1,0:T(8,128)S(1)} %copy-done.6, ...), channel_id=1, replica_groups=mesh['groups'=2,'seq'=8,'head'=1,'sub'=2] {'seq','sub'}, use_global_device_ids=true, to_apply=%region_9.0 | all-reduce | flops 12312 | bytes 98496 | tf_op jit(solution)/shard_map/psum | solution.py:95
  554.5 57.7 %all-reduce = (f32[8,512]{1,0:T(8,128)S(1)}, f32[8,512]{1,0:T(8,128)S(1)}, f32[8,512]{1,0:T(8,128)S(1)}) all-reduce(f32[8,512]{1,0:T(8,128)S(1)} %multiply_reduce_fusion, f32[8,512]{1,0:T(8,128)S(1)} %get-tuple-element.24, f32[8,512]{1,0:T(8,128)S(1)} %get-tuple-element.23), channel_id=1, replica_groups=mesh['groups'=2,'seq'=8,'head'=1,'sub'=2] {'seq','sub'}, use_global_device_ids=true, to_apply=%region_21.0 | all-reduce | flops 12288 | bytes 98304 | tf_op jit(solution)/shard_map/psum | solution.py:104
  619.0 4.4 collective-permute-start.1
  623.5 8.6 %collective-permute-done = bf16[8,32,512]{2,1,0:T(8,128)(2,1)S(1)} collective-permute-done((bf16[8,32,512]{2,1,0:T(8,128)(2,1)S(1)}, bf16[8,32,512]{2,1,0:T(8,128)(2,1)S(1)}, u32[]{:S(2)}, u32[]{:S(2)}) %collective-permute-start) | collective-permute-done | bytes 262176 | tf_op jit(solution)/shard_map/ppermute | solution.py:21
  632.1 4.4 collective-permute-start.3
  636.5 4.2 collective-permute-done.2
  640.7 4.4 collective-permute-start.5
  645.1 9.3 %collective-permute-done.4 = bf16[8,32,512]{2,1,0:T(8,128)(2,1)S(1)} collective-permute-done((bf16[8,32,512]{2,1,0:T(8,128)(2,1)S(1)}, bf16[8,32,512]{2,1,0:T(8,128)(2,1)S(1)}, u32[]{:S(2)}, u32[]{:S(2)}) %collective-permute-start.4) | collective-permute-done | bytes 262176 | tf_op jit(solution)/shard_map/ppermute | solution.py:21
  655.2 4.5 collective-permute-start.7
  660.4 4.1 collective-permute-done.6
  668.6 4.6 collective-permute-start.9
  677.1 4.7 collective-permute-start.11
  686.1 4.6 collective-permute-start.13
  694.2 4.8 collective-permute-done.13
  699.8 3.0 collective-permute-done.14
  703.6 15.5 %fusion.10 = f32[8,512,1024]{1,2,0:T(8,128)} fusion(bf16[8,1024,512]{2,1,0:T(8,128)(2,1)} %param.7, bf16[8,512,512]{2,0,1:T(8,128)(2,1)} %all-gather.12.cloned.1.call-done), kind=kOutput, calls=%fused_computation.18 | convolution fusion | flops 4294967296 | bytes 29360128 | tf_op jit(solution)/shard_map/htd,hdf->htf/dot_general | solution.py:48
  719.0 10.8 %all-gather.14.cloned.1.call-done = bf16[8,512,512]{2,0,1:T(8,128)(2,1)} async-done(((bf16[8,32,512]{2,0,1:T(8,128)(2,1)}), bf16[8,512,512]{2,0,1:T(8,128)(2,1)}) %all-gather.14.cloned.1.call-update) | async-done | bytes 4194320 | tf_op jit(solution)/shard_map/all_gather | solution.py:114
  729.8 22.5 %convolution_convert_fusion = bf16[8,1024,512]{2,1,0:T(8,128)(2,1)} fusion(bf16[8,512,512]{2,1,0:T(8,128)(2,1)} %constant_dynamic-update-slice_fusion, f32[8,512,1024]{1,2,0:T(8,128)} %fusion.10, bf16[8,1024,512]{2,1,0:T(8,128)(2,1)} %param.7, bf16[8,512,512]{2,0,1:T(8,128)(2,1)} %all-gather.14.cloned.1.call-done), kind=kOutput, calls=%fused_computation.16 | convolution fusion | flops 8619294720 | bytes 41943040 | tf_op jit(solution)/shard_map/htf,hfd->htd/dot_general | solution.py:51
  (86 shorter events, 42.0 us)
Async XLA Ops:
  6.5 56.3 %all-gather.10.cloned.1.call-start = ((), (), s32[]{:S(2)}) async-start(), calls=%async_computation.5 | async-start | bytes 4456448 | tf_op jit(solution)/shard_map/all_gather | solution.py:76
  9.1 105.0 %all-gather.6.cloned.1.call-start = ((), (), s32[]{:S(2)}) async-start(), calls=%async_computation.3 | async-start | bytes 4456448 | tf_op jit(solution)/shard_map/all_gather | solution.py:78
  11.8 153.7 %all-gather.8.cloned.1.call-start = ((), (), s32[]{:S(2)}) async-start(), calls=%async_computation.4 | async-start | bytes 4456448 | tf_op jit(solution)/shard_map/all_gather | solution.py:77
  14.5 258.1 %reduce-scatter.6.cloned.1.call-start = ((), (), s32[]{:S(2)}) async-start(), calls=%async_computation.7 | async-start | bytes 8912896 | tf_op jit(solution)/shard_map/reduce_scatter | solution.py:83
  155.8 225.2 %reduce-scatter.8.cloned.1.call-start = ((), (), s32[]{:S(2)}) async-start(), calls=%async_computation.8 | async-start | bytes 8912896 | tf_op jit(solution)/shard_map/reduce_scatter | solution.py:84
  203.8 285.5 %reduce-scatter.4.cloned.1.call-start = ((), (), s32[]{:S(2)}) async-start(), calls=%async_computation.6 | async-start | bytes 8912896 | tf_op jit(solution)/shard_map/reduce_scatter | solution.py:82
  239.9 250.7 %copy-start.5 = (f32[8,512]{1,0:T(8,128)S(1)}, f32[8,512]{1,0:T(8,128)}, u32[]{:S(2)}) copy-start(f32[8,512]{1,0:T(8,128)} %get-tuple-element.16) | copy-start | bytes 49156
  239.9 250.7 %copy-start.6 = (f32[8,512]{1,0:T(8,128)S(1)}, f32[8,512]{1,0:T(8,128)}, u32[]{:S(2)}) copy-start(f32[8,512]{1,0:T(8,128)} %get-tuple-element.18) | copy-start | bytes 49156
  239.9 250.7 %copy-start.7 = (f32[8,512]{1,0:T(8,128)S(1)}, f32[8,512]{1,0:T(8,128)}, u32[]{:S(2)}) copy-start(f32[8,512]{1,0:T(8,128)} %get-tuple-element.14) | copy-start | bytes 49156
  239.9 311.4 %copy-start.2 = (f32[8,32,512]{2,1,0:T(8,128)S(1)}, f32[8,32,512]{2,1,0:T(8,128)}, u32[]{:S(2)}) copy-start(f32[8,32,512]{2,1,0:T(8,128)} %param.13) | copy-start | bytes 1572868
  239.9 312.7 %copy-start = (f32[8,32,512]{2,1,0:T(8,128)S(1)}, f32[8,32,512]{2,1,0:T(8,128)}, u32[]{:S(2)}) copy-start(f32[8,32,512]{2,1,0:T(8,128)} %param.11) | copy-start | bytes 1572868
  240.0 312.7 %copy-start.1 = (f32[8,32,512]{2,1,0:T(8,128)S(1)}, f32[8,32,512]{2,1,0:T(8,128)}, u32[]{:S(2)}) copy-start(f32[8,32,512]{2,1,0:T(8,128)} %param.12) | copy-start | bytes 1572868
  240.0 463.6 %all-gather.12.cloned.1.call-start = ((), (), s32[]{:S(2)}) async-start(), calls=%async_computation.9 | async-start | bytes 4456448 | tf_op jit(solution)/shard_map/all_gather | solution.py:113
  381.0 236.0 %copy-start.3 = (f32[8,32,512]{2,1,0:T(8,128)S(1)}, f32[8,32,512]{2,1,0:T(8,128)}, u32[]{:S(2)}) copy-start(f32[8,32,512]{2,1,0:T(8,128)} %reduce-scatter.8.cloned.1.call-done) | copy-start | bytes 1572868
  614.4 115.5 %all-gather.14.cloned.1.call-start = ((), (), s32[]{:S(2)}) async-start(), calls=%async_computation.10 | async-start | bytes 4456448 | tf_op jit(solution)/shard_map/all_gather | solution.py:114
  617.1 1.9 copy-start.4
  619.0 13.0 %collective-permute-start = (bf16[8,32,512]{2,1,0:T(8,128)(2,1)S(1)}, bf16[8,32,512]{2,1,0:T(8,128)(2,1)S(1)}, u32[]{:S(2)}, u32[]{:S(2)}) collective-permute-start(bf16[8,32,512]{2,1,0:T(8,128)(2,1)S(1)} %get-tuple-element.13), channel_id=1, source_target_pairs={{0,1},{1,2},{2,3},{3,4},{4,5},{5,6},{6,7},{7,8},{8,9},{9,10},{10,1... | collective-permute-start | bytes 786440 | tf_op jit(solution)/shard_map/ppermute | solution.py:21
  619.0 13.0 %collective-permute-start.1 = (bf16[8,32,512]{2,1,0:T(8,128)(2,1)S(1)}, bf16[8,32,512]{2,1,0:T(8,128)(2,1)S(1)}, u32[]{:S(2)}, u32[]{:S(2)}) collective-permute-start(bf16[8,32,512]{2,1,0:T(8,128)(2,1)S(1)} %get-tuple-element.13), channel_id=1, source_target_pairs={{0,15},{1,0},{2,1},{3,2},{4,3},{5,4},{6,5},{7,6},{8,7},{9,8},{10,9... | collective-permute-start | bytes 786440 | tf_op jit(solution)/shard_map/ppermute | solution.py:26
  632.1 8.6 %collective-permute-start.2 = (bf16[8,32,512]{2,1,0:T(8,128)(2,1)S(1)}, bf16[8,32,512]{2,1,0:T(8,128)(2,1)S(1)}, u32[]{:S(2)}, u32[]{:S(2)}) collective-permute-start(bf16[8,32,512]{2,1,0:T(8,128)(2,1)S(1)} %collective-permute-done), channel_id=1, source_target_pairs={{0,1},{1,2},{2,3},{3,4},{4,5},{5,6},{6,7},{7,8},{8,9},{9,10},{10,1... | collective-permute-start | bytes 786440 | tf_op jit(solution)/shard_map/ppermute | solution.py:21
  632.1 8.6 %collective-permute-start.3 = (bf16[8,32,512]{2,1,0:T(8,128)(2,1)S(1)}, bf16[8,32,512]{2,1,0:T(8,128)(2,1)S(1)}, u32[]{:S(2)}, u32[]{:S(2)}) collective-permute-start(bf16[8,32,512]{2,1,0:T(8,128)(2,1)S(1)} %collective-permute-done.1), channel_id=1, source_target_pairs={{0,15},{1,0},{2,1},{3,2},{4,3},{5,4},{6,5},{7,6},{8,7},{9,8},{10,9... | collective-permute-start | bytes 786440 | tf_op jit(solution)/shard_map/ppermute | solution.py:26
  640.7 13.8 %collective-permute-start.4 = (bf16[8,32,512]{2,1,0:T(8,128)(2,1)S(1)}, bf16[8,32,512]{2,1,0:T(8,128)(2,1)S(1)}, u32[]{:S(2)}, u32[]{:S(2)}) collective-permute-start(bf16[8,32,512]{2,1,0:T(8,128)(2,1)S(1)} %collective-permute-done.2), channel_id=1, source_target_pairs={{0,1},{1,2},{2,3},{3,4},{4,5},{5,6},{6,7},{7,8},{8,9},{9,10},{10,1... | collective-permute-start | bytes 786440 | tf_op jit(solution)/shard_map/ppermute | solution.py:21
  640.7 14.5 %collective-permute-start.5 = (bf16[8,32,512]{2,1,0:T(8,128)(2,1)S(1)}, bf16[8,32,512]{2,1,0:T(8,128)(2,1)S(1)}, u32[]{:S(2)}, u32[]{:S(2)}) collective-permute-start(bf16[8,32,512]{2,1,0:T(8,128)(2,1)S(1)} %collective-permute-done.3), channel_id=1, source_target_pairs={{0,15},{1,0},{2,1},{3,2},{4,3},{5,4},{6,5},{7,6},{8,7},{9,8},{10,9... | collective-permute-start | bytes 786440 | tf_op jit(solution)/shard_map/ppermute | solution.py:26
  654.4 10.1 %collective-permute-start.6 = (bf16[8,32,512]{2,1,0:T(8,128)(2,1)S(1)}, bf16[8,32,512]{2,1,0:T(8,128)(2,1)S(1)}, u32[]{:S(2)}, u32[]{:S(2)}) collective-permute-start(bf16[8,32,512]{2,1,0:T(8,128)(2,1)S(1)} %collective-permute-done.4), channel_id=1, source_target_pairs={{0,1},{1,2},{2,3},{3,4},{4,5},{5,6},{6,7},{7,8},{8,9},{9,10},{10,1... | collective-permute-start | bytes 786440 | tf_op jit(solution)/shard_map/ppermute | solution.py:21
  655.2 13.4 %collective-permute-start.7 = (bf16[8,32,512]{2,1,0:T(8,128)(2,1)S(1)}, bf16[8,32,512]{2,1,0:T(8,128)(2,1)S(1)}, u32[]{:S(2)}, u32[]{:S(2)}) collective-permute-start(bf16[8,32,512]{2,1,0:T(8,128)(2,1)S(1)} %collective-permute-done.5), channel_id=1, source_target_pairs={{0,15},{1,0},{2,1},{3,2},{4,3},{5,4},{6,5},{7,6},{8,7},{9,8},{10,9... | collective-permute-start | bytes 786440 | tf_op jit(solution)/shard_map/ppermute | solution.py:26
  664.5 9.7 %collective-permute-start.8 = (bf16[8,32,512]{2,1,0:T(8,128)(2,1)S(1)}, bf16[8,32,512]{2,1,0:T(8,128)(2,1)S(1)}, u32[]{:S(2)}, u32[]{:S(2)}) collective-permute-start(bf16[8,32,512]{2,1,0:T(8,128)(2,1)S(1)} %collective-permute-done.6), channel_id=1, source_target_pairs={{0,1},{1,2},{2,3},{3,4},{4,5},{5,6},{6,7},{7,8},{8,9},{9,10},{10,1... | collective-permute-start | bytes 786440 | tf_op jit(solution)/shard_map/ppermute | solution.py:21
  668.6 8.5 %collective-permute-start.9 = (bf16[8,32,512]{2,1,0:T(8,128)(2,1)S(1)}, bf16[8,32,512]{2,1,0:T(8,128)(2,1)S(1)}, u32[]{:S(2)}, u32[]{:S(2)}) collective-permute-start(bf16[8,32,512]{2,1,0:T(8,128)(2,1)S(1)} %collective-permute-done.7), channel_id=1, source_target_pairs={{0,15},{1,0},{2,1},{3,2},{4,3},{5,4},{6,5},{7,6},{8,7},{9,8},{10,9... | collective-permute-start | bytes 786440 | tf_op jit(solution)/shard_map/ppermute | solution.py:26
  674.2 8.5 %collective-permute-start.10 = (bf16[8,32,512]{2,1,0:T(8,128)(2,1)S(1)}, bf16[8,32,512]{2,1,0:T(8,128)(2,1)S(1)}, u32[]{:S(2)}, u32[]{:S(2)}) collective-permute-start(bf16[8,32,512]{2,1,0:T(8,128)(2,1)S(1)} %collective-permute-done.8), channel_id=1, source_target_pairs={{0,1},{1,2},{2,3},{3,4},{4,5},{5,6},{6,7},{7,8},{8,9},{9,10},{10,1... | collective-permute-start | bytes 786440 | tf_op jit(solution)/shard_map/ppermute | solution.py:21
  677.1 9.0 %collective-permute-start.11 = (bf16[8,32,512]{2,1,0:T(8,128)(2,1)S(1)}, bf16[8,32,512]{2,1,0:T(8,128)(2,1)S(1)}, u32[]{:S(2)}, u32[]{:S(2)}) collective-permute-start(bf16[8,32,512]{2,1,0:T(8,128)(2,1)S(1)} %collective-permute-done.9), channel_id=1, source_target_pairs={{0,15},{1,0},{2,1},{3,2},{4,3},{5,4},{6,5},{7,6},{8,7},{9,8},{10,9... | collective-permute-start | bytes 786440 | tf_op jit(solution)/shard_map/ppermute | solution.py:26
  682.7 10.0 %collective-permute-start.12 = (bf16[8,32,512]{2,1,0:T(8,128)(2,1)S(1)}, bf16[8,32,512]{2,1,0:T(8,128)(2,1)S(1)}, u32[]{:S(2)}, u32[]{:S(2)}) collective-permute-start(bf16[8,32,512]{2,1,0:T(8,128)(2,1)S(1)} %collective-permute-done.10), channel_id=1, source_target_pairs={{0,1},{1,2},{2,3},{3,4},{4,5},{5,6},{6,7},{7,8},{8,9},{9,10},{10,1... | collective-permute-start | bytes 786440 | tf_op jit(solution)/shard_map/ppermute | solution.py:21
  686.1 13.0 %collective-permute-start.13 = (bf16[8,32,512]{2,1,0:T(8,128)(2,1)S(1)}, bf16[8,32,512]{2,1,0:T(8,128)(2,1)S(1)}, u32[]{:S(2)}, u32[]{:S(2)}) collective-permute-start(bf16[8,32,512]{2,1,0:T(8,128)(2,1)S(1)} %collective-permute-done.11), channel_id=1, source_target_pairs={{0,15},{1,0},{2,1},{3,2},{4,3},{5,4},{6,5},{7,6},{8,7},{9,8},{10,9... | collective-permute-start | bytes 786440 | tf_op jit(solution)/shard_map/ppermute | solution.py:26
  692.7 10.2 %collective-permute-start.14 = (bf16[8,32,512]{2,1,0:T(8,128)(2,1)S(1)}, bf16[8,32,512]{2,1,0:T(8,128)(2,1)S(1)}, u32[]{:S(2)}, u32[]{:S(2)}) collective-permute-start(bf16[8,32,512]{2,1,0:T(8,128)(2,1)S(1)} %collective-permute-done.12), channel_id=1, source_target_pairs={{0,1},{1,2},{2,3},{3,4},{4,5},{5,6},{6,7},{7,8},{8,9},{9,10},{10,1... | collective-permute-start | bytes 786440 | tf_op jit(solution)/shard_map/ppermute | solution.py:21
Sparse Core Ops, SparseCore 0:
  9.5 53.2 all-gather.9
  65.0 49.0 all-gather.5
  116.3 49.0 all-gather.7
  169.4 103.1 reduce-scatter.5
  276.5 104.4 reduce-scatter.7
  384.9 104.3 reduce-scatter.3
  614.5 58.8 all-gather.11
  675.5 54.2 all-gather.13
